TPU v7x, 32 devices: a whole 2x2x4 slice. The times are simulated.
32 devices in a mesh: row: 4 (over y, x), col: 8 (over z, core).
Axes of the slice: x: 2, y: 2, z: 4, core: 2. Of those that a mesh axis runs over, the one named last changes fastest.
Arguments:
- factor_diag: float32 [2, 512, 512], replicated, as said below
- factor_mid: float32 [512, 512], replicated, may hold values from -0.25 to 0.25
- factor_low: float32 [2, 16384, 512], P(None, ('row', 'col')), may hold values from -0.046875 to 0.046875
- adjoint_diag: float32 [2, 512, 512], replicated, may hold values from -6 to 6
- adjoint_mid: float32 [512, 512], replicated, may hold values from -6 to 6
- adjoint_low: float32 [2, 16384, 512], P(None, ('row', 'col')), may hold values from -6 to 6
- trailing_adjoint: float32 [16384, 4, 4096], P('row', None, 'col'), as said below
Outputs:
- grad_diag: float32 [2, 512, 512], replicated
- grad_mid: float32 [512, 512], replicated
- grad_low: float32 [2, 16384, 512], P(None, ('row', 'col'))
Inputs may be any that keep to these rules, and one draw needn't show every extreme that they name: `factor_diag`: each of the two [512, 512] blocks is lower triangular with diagonal entries between 1 and 2. `trailing_adjoint`: symmetric when read as an 16384 x 16384 matrix in row-major order.
All inputs are finite; a program needn't handle non-finite values.
Results may differ from a plain program's by a relative error of at most 0.000065.
Values sent between devices are 32-bit elements; how exact they have to be, the bound alone decides.
A program may use at most 192 MiB of HBM per device.

v0:
```python
import jax
import jax.numpy as jnp
from jax import lax
from jax.sharding import PartitionSpec as P


def lower_half(matrix):
    return jnp.tril(matrix, -1) + 0.5 * jnp.diag(jnp.diag(matrix))


def product(left_side, right_side):
    return jnp.dot(
        left_side, right_side, precision=lax.Precision.HIGHEST, preferred_element_type=jnp.float32
    )


def right_solve(factor, row_block):
    return jax.scipy.linalg.solve_triangular(factor, row_block.T, trans=1, lower=True).T


def diag_adjoint(factor, adjoint):
    inner_term = lower_half(product(factor.T, adjoint))
    halfway = jax.scipy.linalg.solve_triangular(factor, inner_term, trans=1, lower=True)
    whole_term = right_solve(factor, halfway)
    return 0.5 * (whole_term + whole_term.T)


def shards(
    factor_diag, factor_mid, factor_low, adjoint_diag, adjoint_mid, adjoint_low, trailing_adjoint
):
    block_rows, row_groups, group_cols = trailing_adjoint.shape
    local_block = trailing_adjoint.reshape(block_rows, row_groups * group_cols)

    def image_of(panel):
        columns = lax.all_gather(panel, "row", axis=0, tiled=True)
        return lax.psum_scatter(
            product(local_block, columns), "col", scatter_dimension=0, tiled=True
        )

    second_image = image_of(factor_low[1])
    first_image = image_of(factor_low[0])
    second_solved = right_solve(factor_diag[1], adjoint_low[1] - 2.0 * second_image)
    second_total = lax.psum(product(second_solved.T, factor_low[1]), ("row", "col"))
    second_grad = diag_adjoint(factor_diag[1], adjoint_diag[1] - second_total)
    second_half = 0.5 * second_solved
    upper_term = product(second_half.T, factor_low[0])
    bottom_rows = adjoint_low[0] - 2.0 * (product(second_half, factor_mid) + first_image)
    bottom_solved = right_solve(factor_diag[0], bottom_rows)
    lower_term = product(bottom_solved.T, factor_low[0])
    upper_total = lax.psum(upper_term, ("row", "col"))
    lower_total = lax.psum(lower_term, ("row", "col"))
    top_rows = adjoint_mid - 2.0 * (product(second_grad, factor_mid) + upper_total)
    top_solved = right_solve(factor_diag[0], top_rows)
    first_adjoint = adjoint_diag[0] - product(top_solved.T, factor_mid) - lower_total
    first_grad = diag_adjoint(factor_diag[0], first_adjoint)
    return (
        jnp.stack([first_grad, second_grad]),
        0.5 * top_solved,
        jnp.stack([0.5 * bottom_solved, second_half]),
    )


def solution(mesh):
    return jax.shard_map(
        shards,
        mesh=mesh,
        in_specs=(
            P(),
            P(),
            P(None, ("row", "col"), None),
            P(),
            P(),
            P(None, ("row", "col"), None),
            P("row", None, "col"),
        ),
        out_specs=(P(), P(), P(None, ("row", "col"), None)),
        check_vma=False,
    )
```

profile of v0, /device:TPU:0, one launch (start us, length us, event | category | flops | bytes accessed | tf_op | source)
XLA Modules:
  0.0 540.5 jit_solution(1734141429573392503)
XLA Ops:
  7.2 3.1 fusion.165
  11.2 30.0 %copy.24 = f32[512,8,4,512]{3,1,2,0:T(8,128)} copy(f32[512,8,4,512]{3,2,1,0:T(4,128)} %bitcast.203) | data formatting | bytes 67108864
  41.2 24.7 %all-gather.5.cloned.1.call-done = f32[1,2048,512]{2,1,0:T(8,128)} async-done(((f32[1,512,512]{2,1,0:T(8,128)}), f32[1,2048,512]{2,1,0:T(8,128)}) %all-gather.5.cloned.1.call-update) | async-done | bytes 4194320 | tf_op jit(solution)/shard_map/all_gather | solution.py:35
  65.9 65.0 %fusion.2 = f32[4096,512]{1,0:T(8,128)} fusion(f32[4096,2048]{1,0:T(8,128)} %bitcast.204, f32[1,2048,512]{2,1,0:T(8,128)} %all-gather.5.cloned.1.call-done), kind=kOutput, calls=%fused_computation.8 | convolution fusion | flops 51539607552 | bytes 46137344 | tf_op jit(solution)/shard_map/dot_general | solution.py:12
  131.0 65.1 %fusion = f32[4096,512]{1,0:T(8,128)} fusion(f32[4096,2048]{1,0:T(8,128)} %bitcast.205, f32[1,2048,512]{2,1,0:T(8,128)} %all-gather.7.cloned.1.call-done), kind=kOutput, calls=%fused_computation.6 | convolution fusion | flops 51539607552 | bytes 46137344 | tf_op jit(solution)/shard_map/dot_general | solution.py:12
  199.2 11.8 %while.14 = (s32[]{:T(128)}, f32[512,512]{1,0:T(8,128)}, s32[4,2]{0,1:T(2,128)S(1)}, f32[4,128,128]{2,1,0:T(8,128)S(1)}, s32[]{:T(128)}) while((s32[]{:T(128)}, f32[512,512]{1,0:T(8,128)}, s32[4,2]{0,1:T(2,128)S(1)}, f32[4,128,128]{2,1,0:T(8,128)S(1)}, s32[]{:T(128)}) %tuple.60), condition=%wide.while_cond.clone.1, body=%wide.while_body.clone.1.sunk | while | flops 2 | bytes 131181 | solution.py:18
  199.9 2.3 bitcast_dynamic-update-slice_fusion.4
  202.9 2.3 bitcast_dynamic-update-slice_fusion.4
  205.8 2.3 bitcast_dynamic-update-slice_fusion.4
  208.8 2.2 bitcast_dynamic-update-slice_fusion.4
  211.0 39.3 %custom-call.15 = f32[4,128,128]{1,2,0:T(8,128)S(1)} custom-call(f32[4,128,128]{2,1,0:T(8,128)S(1)} %get-tuple-element.50), custom_call_target="InvertDiagBlocksLowerTriangular" | custom-call | tf_op jit(solution)/shard_map/jit(_solve_triangular)/triangular_solve | solution.py:18
  250.4 11.3 %while.15 = (s32[]{:T(128)}, f32[512,512]{1,0:T(8,128)}, s32[4,2]{0,1:T(2,128)S(1)}, f32[4,128,128]{2,1,0:T(8,128)S(1)}, s32[]{:T(128)}) while((s32[]{:T(128)}, f32[512,512]{1,0:T(8,128)}, s32[4,2]{0,1:T(2,128)S(1)}, f32[4,128,128]{2,1,0:T(8,128)S(1)}, s32[]{:T(128)}) %tuple.77), condition=%wide.while_cond.clone.5, body=%wide.while_body.clone.5.sunk | while | flops 2 | bytes 131181 | solution.py:18
  251.0 2.2 bitcast_dynamic-update-slice_fusion.5
  253.8 2.2 bitcast_dynamic-update-slice_fusion.5
  261.7 39.9 %custom-call.19 = f32[4,128,128]{1,2,0:T(8,128)} custom-call(f32[4,128,128]{2,1,0:T(8,128)S(1)} %get-tuple-element.54), custom_call_target="InvertDiagBlocksLowerTriangular" | custom-call | tf_op jit(solution)/shard_map/jit(_solve_triangular)/triangular_solve | solution.py:18
  309.1 2.5 convolution_subtract_fusion.21
  312.1 2.8 fusion.13
  314.9 2.8 fusion.15
  317.7 3.8 fusion.10
  323.8 2.4 convolution_subtract_fusion.5
  326.6 2.5 convolution_subtract_fusion.17
  330.3 2.8 fusion.11
  336.8 135.3 %all-reduce.3.cloned.1.call-done = (f32[512,512]{1,0:T(8,128)}, f32[512,512]{1,0:T(8,128)}, f32[512,512]{1,0:T(8,128)}) async-done(((f32[512,512]{1,0:T(8,128)}, f32[512,512]{1,0:T(8,128)}, f32[512,512]{1,0:T(8,128)}), (f32[512,512]{1,0:T(8,128)}, f32[512,512]{1,0:T(8,128)}, f32[512,512]{1,0:T(8,128)})) %all-reduce.3.cloned.1.call-update) | async-done | bytes 3145744 | tf_op jit(solution)/shard_map/psum | solution.py:43
  472.0 3.7 convolution_bitcast_fusion.1
  475.8 4.7 gather_fusion
  486.6 2.4 convolution_subtract_fusion.19
  492.1 3.9 fusion.8
  500.5 2.6 convolution_subtract_fusion.18
  504.6 2.5 copy.20
  507.1 3.6 fusion.5
  512.7 4.5 gather_fusion.1
  527.7 2.6 copy.19
  (159 shorter events, 59.2 us)
Async XLA Ops:
  7.2 310.6 %copy-start = (f32[512,512]{1,0:T(8,128)S(1)}, f32[512,512]{1,0:T(8,128)}, u32[]{:S(2)}) copy-start(f32[512,512]{1,0:T(8,128)} %param.10) | copy-start | bytes 3145732
  7.2 58.7 %all-gather.5.cloned.1.call-start = ((), (), s32[]{:S(2)}) async-start(), calls=%async_computation.4 | async-start | bytes 5242880 | tf_op jit(solution)/shard_map/all_gather | solution.py:35
  10.4 120.6 %all-gather.7.cloned.1.call-start = ((), (), s32[]{:S(2)}) async-start(), calls=%async_computation.5 | async-start | bytes 5242880 | tf_op jit(solution)/shard_map/all_gather | solution.py:35
  11.1 290.5 %reduce-scatter.3.cloned.1.call-start = ((), (), s32[]{:S(2)}) async-start(), calls=%async_computation.2 | async-start | bytes 9437184 | tf_op jit(solution)/shard_map/reduce_scatter | solution.py:36
  130.9 186.8 %reduce-scatter.5.cloned.1.call-start = ((), (), s32[]{:S(2)}) async-start(), calls=%async_computation.3 | async-start | bytes 9437184 | tf_op jit(solution)/shard_map/reduce_scatter | solution.py:36
  196.1 1.6 copy-start.10
  196.1 275.9 %all-reduce.3.cloned.1.call-start = ((), (), s32[]{:S(2)}) async-start(), calls=%async_computation.6 | async-start | bytes 6291456 | tf_op jit(solution)/shard_map/psum | solution.py:43
  250.3 53.1 %copy-start.25 = (f32[4,128,128]{1,2,0:T(8,128)}, f32[4,128,128]{1,2,0:T(8,128)S(1)}, u32[]{:S(2)}) copy-start(f32[4,128,128]{1,2,0:T(8,128)S(1)} %custom-call.15) | copy-start | bytes 786436
  303.8 4.9 copy-start.26
  305.3 6.7 %copy-start.1 = (f32[2,512,512]{2,1,0:T(8,128)S(1)}, f32[2,512,512]{2,1,0:T(8,128)}, u32[]{:S(2)}) copy-start(f32[2,512,512]{2,1,0:T(8,128)} %param.11) | copy-start | bytes 6291460
  306.7 8.2 %copy-start.2 = (f32[128,512]{1,0:T(8,128)}, f32[128,512]{1,0:T(8,128)S(1)}, u32[]{:S(2)}) copy-start(f32[128,512]{1,0:T(8,128)S(1)} %fusion.121) | copy-start | bytes 786436
  309.1 5.8 %copy-start.4 = (f32[128,512]{1,0:T(8,128)}, f32[128,512]{1,0:T(8,128)S(1)}, u32[]{:S(2)}) copy-start(f32[128,512]{1,0:T(8,128)S(1)} %fusion.118) | copy-start | bytes 786436
  312.0 2.8 copy-start.13
  317.7 3.8 copy-start.18
  321.9 7.6 %copy-start.6 = (f32[128,512]{1,0:T(8,128)}, f32[128,512]{1,0:T(8,128)S(1)}, u32[]{:S(2)}) copy-start(f32[128,512]{1,0:T(8,128)S(1)} %fusion.89) | copy-start | bytes 786436
  323.8 5.7 %copy-start.15 = (f32[128,512]{1,0:T(8,128)}, f32[128,512]{1,0:T(8,128)S(1)}, u32[]{:S(2)}) copy-start(f32[128,512]{1,0:T(8,128)S(1)} %fusion.135) | copy-start | bytes 786436
  326.6 2.9 copy-start.21
  333.1 1.1 copy-start.7
  333.1 1.2 copy-start.14
  333.1 1.3 copy-start.16
  333.1 1.3 copy-start.22
  333.1 1.4 copy-start.29
  475.8 4.9 copy-start.27
  475.8 5.3 copy-start.17
  489.4 2.6 copy-start.23
  492.1 3.9 copy-start.8
  492.1 3.9 copy-start.19
  507.1 3.6 copy-start.11
  517.3 1.2 copy-start.12
  520.8 1.4 copy-start.20
  524.1 1.9 copy-start.24
  526.7 3.6 copy-start.9
  (4 other events, 3.4 us)
Sparse Core Ops, SparseCore 0:
  10.5 55.3 all-gather.4
  68.3 52.6 all-gather.6
  131.0 89.7 reduce-scatter.2
  223.0 87.9 reduce-scatter.4
  333.3 138.7 all-reduce.2
where the time goes:
time: 549 us; the launch traced here: 540 us
  matrix products  195 us (36%)
  waiting for transfers between devices  161 us (29%)
  other arithmetic  90.2 us (16%)
  local copies, waits for them, and re-layouts  78.6 us (14%)
  between operations  14.9 us (3%)
    dot_general x10, matrix products, product(): jnp.dot(left_side, right_side, precision=lax.Precision.HIGHEST, preferred...  155 us
    psum x1, waiting for transfers between devices, shards(): lax.psum(product(second_solved.T, factor_low[1]), ('row', 'col'))  135 us
    another operation x4, other arithmetic, right_solve(): jax.scipy.linalg.solve_triangular(factor, row_block.T, trans=1, lower=True)  80.8 us
    unnamed x65, local copies, waits for them, and re-layouts  39.2 us
    another operation x35, matrix products, right_solve(): jax.scipy.linalg.solve_triangular(factor, row_block.T, trans=1, lower=True)  33.9 us
    all_gather x2, waiting for transfers between devices, image_of(): columns = lax.all_gather(panel, 'row', axis=0, tiled=True)  24.7 us
    another operation x27, local copies, waits for them, and re-layouts, right_solve(): jax.scipy.linalg.solve_triangular(factor, row_block.T, trans=1, lower=True)  22.9 us
  transfers between devices with their start and end apart: 5, of which 2 were waited for; matrix products, arithmetic and copies ran while one was open for 52% of the time, Pallas kernels for 0%

commit v1 on v0

v1 whole, which is shorter than its diff:
```python
import jax
import jax.numpy as jnp
from jax import lax
from jax.sharding import PartitionSpec as P

LEAF = 128


def product(left_side, right_side, precision=lax.Precision.HIGHEST):
    return jnp.matmul(
        left_side, right_side, precision=precision, preferred_element_type=jnp.float32
    )


def cross(left_side, right_side, precision=lax.Precision.HIGHEST):
    return lax.dot_general(
        left_side,
        right_side,
        (((0,), (0,)), ((), ())),
        precision=precision,
        preferred_element_type=jnp.float32,
    )


def lower_half(matrix):
    rows = lax.broadcasted_iota(jnp.int32, matrix.shape, 0)
    cols = lax.broadcasted_iota(jnp.int32, matrix.shape, 1)
    return jnp.where(rows > cols, matrix, jnp.where(rows == cols, 0.5 * matrix, 0.0))


def lower_inverse(factors):
    count, order, _ = factors.shape
    leaf = min(LEAF, order)
    blocks = jnp.stack(
        [factors[:, i : i + leaf, i : i + leaf] for i in range(0, order, leaf)], axis=1
    ).reshape(-1, leaf, leaf)
    rows = lax.broadcasted_iota(jnp.int32, (leaf, leaf), 0)
    cols = lax.broadcasted_iota(jnp.int32, (leaf, leaf), 1)
    inverse = jnp.where(rows == cols, 1.0 / jnp.where(rows == cols, blocks, 1.0), 0.0)
    size = 1
    while size < leaf:
        corner = (rows // (2 * size) == cols // (2 * size)) & (rows // size > cols // size)
        inner = jnp.where(corner, blocks, 0.0)
        inverse = inverse - product(product(inverse, inner), inverse)
        size *= 2
    pieces = inverse.reshape(count, order // leaf, leaf, leaf)
    while size < order:
        pairs = order // (2 * size)
        first, second = pieces[:, 0::2], pieces[:, 1::2]
        corner = jnp.stack(
            [
                factors[:, (2 * i + 1) * size : (2 * i + 2) * size, 2 * i * size : (2 * i + 1) * size]
                for i in range(pairs)
            ],
            axis=1,
        )
        below = -product(product(second, corner), first)
        pieces = jnp.concatenate(
            [
                jnp.concatenate([first, jnp.zeros_like(first)], axis=3),
                jnp.concatenate([below, second], axis=3),
            ],
            axis=2,
        )
        size *= 2
    return pieces[:, 0]


def swap(value, axis, size, offset):
    return lax.ppermute(value, axis, [(i, i ^ offset) for i in range(size)])


def place(buffer, index, value):
    return lax.dynamic_update_slice_in_dim(buffer, value[None], index, 0)


def pick(buffer, index):
    return lax.dynamic_index_in_dim(buffer, index, 0, keepdims=False)


def gather(value, axis, size, step=1):
    count = size // step
    me = lax.axis_index(axis)
    slot = me // step
    arrived = [swap(value, axis, size, j * step) for j in range(1, count)]
    held = jnp.zeros((count,) + value.shape, value.dtype)
    held = place(held, slot, value)
    for j in range(1, count):
        held = place(held, slot ^ j, arrived[j - 1])
    return held


def scatter(parts, axis, size, step=1):
    count = size // step
    slot = lax.axis_index(axis) // step
    total = pick(parts, slot)
    for j in range(1, count):
        total = total + swap(pick(parts, slot ^ j), axis, size, j * step)
    return total


def total_over(value, n_row, n_col):
    core = lax.axis_index("col") % 2
    halves = value.reshape((2, -1) + value.shape[1:])
    mine = pick(halves, core) + swap(pick(halves, 1 - core), "col", n_col, 1)
    shape = mine.shape
    part = scatter(mine.reshape((n_row, -1) + shape[1:]), "row", n_row)
    part = scatter(part.reshape((n_col // 2, -1) + shape[1:]), "col", n_col, 2)
    part = gather(part, "col", n_col, 2).reshape((-1,) + shape[1:])
    part = gather(part, "row", n_row).reshape(shape)
    other = swap(part, "col", n_col, 1)
    lower = jnp.where(core == 0, part, other)
    upper = jnp.where(core == 0, other, part)
    return jnp.concatenate([lower, upper], axis=0)


def diag_adjoint(factor, inverse, adjoint):
    inner_term = lower_half(cross(factor, adjoint))
    whole_term = product(cross(inverse, inner_term), inverse)
    return 0.5 * (whole_term + whole_term.T)


def solution(mesh):
    n_row, n_col = mesh.shape["row"], mesh.shape["col"]

    def shards(
        factor_diag, factor_mid, factor_low, adjoint_diag, adjoint_mid, adjoint_low, trailing_adjoint
    ):
        block_rows, row_groups, group_cols = trailing_adjoint.shape
        width = factor_mid.shape[0]
        high = lax.Precision.HIGH
        local_block = trailing_adjoint.reshape(block_rows, row_groups * group_cols)
        columns = gather(factor_low[1], "row", n_row).reshape(-1, width)
        chips = gather(factor_low[0], "col", n_col, 2)
        inverses = lower_inverse(factor_diag)
        local_block, columns, chips, inverses = lax.optimization_barrier(
            (local_block, columns, chips, inverses)
        )
        second_image = lax.psum_scatter(
            product(local_block, columns, high), "col", scatter_dimension=0, tiled=True
        )
        core = lax.axis_index("col") % 2
        other = swap(chips, "col", n_col, 1)
        rows = jnp.stack(
            [jnp.where(core == 0, chips, other), jnp.where(core == 0, other, chips)], axis=1
        ).reshape(-1, width)
        partial = cross(local_block, rows, high).reshape(row_groups, group_cols, width)
        first_image = scatter(partial, "row", n_row)

        second_rows = adjoint_low[1] - 2.0 * second_image
        first_rows = adjoint_low[0] - 2.0 * first_image
        terms = jnp.concatenate(
            [
                cross(second_rows, factor_low[1]),
                cross(second_rows, factor_low[0]),
                cross(first_rows, factor_low[0]),
            ],
            axis=0,
        )
        totals = total_over(terms, n_row, n_col)

        second_solved = product(second_rows, inverses[1])
        second_half = 0.5 * second_solved
        bottom_solved = product(first_rows - product(second_solved, factor_mid), inverses[0])

        second_total = cross(inverses[1], totals[:width])
        upper_total = 0.5 * cross(inverses[1], totals[width : 2 * width])
        lower_total = cross(inverses[0], totals[2 * width :] - 2.0 * cross(factor_mid, upper_total))
        second_grad = diag_adjoint(factor_diag[1], inverses[1], adjoint_diag[1] - second_total)
        top_rows = adjoint_mid - 2.0 * (product(second_grad, factor_mid) + upper_total)
        top_solved = product(top_rows, inverses[0])
        first_adjoint = adjoint_diag[0] - cross(top_solved, factor_mid) - lower_total
        first_grad = diag_adjoint(factor_diag[0], inverses[0], first_adjoint)
        return (
            jnp.stack([first_grad, second_grad]),
            0.5 * top_solved,
            jnp.stack([0.5 * bottom_solved, second_half]),
        )

    return jax.shard_map(
        shards,
        mesh=mesh,
        in_specs=(
            P(),
            P(),
            P(None, ("row", "col"), None),
            P(),
            P(),
            P(None, ("row", "col"), None),
            P("row", None, "col"),
        ),
        out_specs=(P(), P(), P(None, ("row", "col"), None)),
        check_vma=False,
    )
```

time: 549 us -> 429 us (0.78)
  other arithmetic: 90.2 us -> 18.9 us
  matrix products: 195 us -> 139 us
  waiting for transfers between devices: 161 us -> 105 us
  starting transfers between devices: 0.38 us -> 38.7 us
  local copies, waits for them, and re-layouts: 78.6 us -> 107 us
    psum x1 -> x0, waiting for transfers between devices: 135 us -> none  [shards(): lax.psum(product(second_solved.T, factor_low[1]), ('row', 'col'))]
    ppermute x0 -> x24, waiting for transfers between devices: none -> 105 us  [swap(): return lax.ppermute(value, axis, [(i, i ^ offset) for i in range(size)])]
    another operation x4 -> x3, other arithmetic: 80.8 us -> 5.57 us  [the longest x2 5.53 us: shards(): jnp.stack([jnp.where(core == 0, chips, other), jnp.where(core == 0, other...]
    another operation x49 -> x0, matrix products: 40 us -> none  [the longest x35 33.9 us: right_solve(): jax.scipy.linalg.solve_triangular(factor, row_block.T, trans=1, lower=True)]
    ppermute x0 -> x24, starting transfers between devices: none -> 38.6 us  [swap(): return lax.ppermute(value, axis, [(i, i ^ offset) for i in range(size)])]
    dot_general x0 -> x3, local copies, waits for them, and re-layouts: none -> 37.3 us  [the longest x1 33.1 us: cross(): lax.dot_general(left_side, right_side, (((0,), (0,)), ((), ())), precisio...]
    all_gather x2 -> x0, waiting for transfers between devices: 24.7 us -> none  [image_of(): columns = lax.all_gather(panel, 'row', axis=0, tiled=True)]
    another operation x27 -> x4, local copies, waits for them, and re-layouts: 22.9 us -> 4.57 us  [right_solve(): jax.scipy.linalg.solve_triangular(factor, row_block.T, trans=1, lower=True)]
  transfers between devices with their start and end apart: 5 -> 25, of which waited for: 2 -> 13; matrix products, arithmetic and copies ran while one was open for 52% -> 39% of each run, Pallas kernels for 0% -> 0%
where the time goes in v1:
time: 429 us; the launch traced here: 424 us
  matrix products  139 us (32%)
  local copies, waits for them, and re-layouts  107 us (25%)
  waiting for transfers between devices  105 us (24%)
  starting transfers between devices  38.7 us (9%)
  other arithmetic  18.9 us (4%)
  between operations  15.1 us (4%)
    ppermute x24, waiting for transfers between devices, swap(): return lax.ppermute(value, axis, [(i, i ^ offset) for i in range(size)])  105 us
    dot_general x13, matrix products, cross(): lax.dot_general(left_side, right_side, (((0,), (0,)), ((), ())), precisio...  75.2 us
    dot_general x26, matrix products, product(): jnp.matmul(left_side, right_side, precision=precision, preferred_element_...  64.1 us
    unnamed x58, local copies, waits for them, and re-layouts  41.6 us
    ppermute x24, starting transfers between devices, swap(): return lax.ppermute(value, axis, [(i, i ^ offset) for i in range(size)])  38.6 us
    dot_general x1, local copies, waits for them, and re-layouts, cross(): lax.dot_general(left_side, right_side, (((0,), (0,)), ((), ())), precisio...  33.1 us
    dynamic_update_slice x14, local copies, waits for them, and re-layouts, place(): return lax.dynamic_update_slice_in_dim(buffer, value[None], index, 0)  12.7 us
  transfers between devices with their start and end apart: 25, of which 13 were waited for; matrix products, arithmetic and copies ran while one was open for 39% of the time, Pallas kernels for 0%

profile of v1, /device:TPU:0, one launch (start us, length us, event | category | flops | bytes accessed | tf_op | source)
XLA Modules:
  0.0 423.8 jit_solution(3765438962968660293)
XLA Ops:
  11.5 3.1 collective-permute-start.3
  14.5 2.6 collective-permute-start.4
  44.4 29.9 %copy.41 = f32[512,8,4,512]{3,1,2,0:T(8,128)} copy(f32[512,8,4,512]{3,2,1,0:T(4,128)} %bitcast.254) | data formatting | bytes 67108864
  78.5 8.2 %collective-permute-done.4 = f32[512,512]{1,0:T(8,128)} collective-permute-done((f32[512,512]{1,0:T(8,128)}, f32[512,512]{1,0:T(8,128)}, u32[]{:S(2)}, u32[]{:S(2)}) %collective-permute-start.4) | collective-permute-done | bytes 1048608 | tf_op jit(solution)/shard_map/ppermute | solution.py:70
  93.9 6.7 %collective-permute-done.2 = f32[512,512]{1,0:T(8,128)S(1)} collective-permute-done((f32[512,512]{1,0:T(8,128)}, f32[512,512]{1,0:T(8,128)S(1)}, u32[]{:S(2)}, u32[]{:S(2)}) %collective-permute-start.2) | collective-permute-done | bytes 1048608 | tf_op jit(solution)/shard_map/ppermute | solution.py:70
  100.7 32.1 %fusion.100 = f32[4096,512]{1,0:T(8,128)} fusion(f32[4096,2048]{1,0:T(8,128)} %bitcast.252, f32[2048,512]{1,0:T(8,128)S(1)} %bitcast.264), kind=kOutput, calls=%fused_computation.230 | convolution fusion | flops 25769803776 | bytes 46137344 | tf_op jit(solution)/shard_map/dot_general | solution.py:10
  132.9 33.1 %copy.27 = f32[2048,4096]{1,0:T(8,128)} copy(f32[2048,4096]{0,1:T(8,128)} %bitcast.253) | data formatting | bytes 67108864 | tf_op jit(solution)/shard_map/dot_general | solution.py:16
  166.1 4.6 %select_bitcast_fusion.1 = (f32[4,1,512,512]{3,2,1,0:T(8,128)S(1)}, f32[4,1,512,512]{3,2,1,0:T(8,128)S(1)}) fusion(f32[4,512,512]{2,1,0:T(8,128)} %bitcast_dynamic-update-slice_fusion, f32[4,512,512]{2,1,0:T(8,128)} %collective-permute-done.6, pred[]{:T(512)S(6)} %eq.50), kind=kLoop, calls=%fused_computation.2 | loop fusion | flops 2097152 | bytes 16777216 | tf_op jit(solution)/shard_map/stack | solution.py:144
  171.6 45.8 %fusion.101 = f32[4,512,512]{2,1,0:T(8,128)S(1)} fusion(f32[4,512,4096]{2,1,0:T(8,128)} %bitcast.255, f32[4096,512,1]{1,0,2:T(8,128)S(1)} %bitcast.258), kind=kOutput, calls=%fused_computation.231 | convolution fusion | flops 25769803776 | bytes 46137344 | tf_op jit(solution)/shard_map/dot_general | solution.py:16
  220.6 3.2 collective-permute-start.9
  223.9 22.8 %collective-permute-done.7 = f32[512,512]{1,0:T(8,128)} collective-permute-done((f32[512,512]{1,0:T(8,128)}, f32[512,512]{1,0:T(8,128)}, u32[]{:S(2)}, u32[]{:S(2)}) %collective-permute-start.7) | collective-permute-done | bytes 1048608 | tf_op jit(solution)/shard_map/ppermute | solution.py:70
  246.7 21.8 %collective-permute-done.8 = f32[512,512]{1,0:T(8,128)} collective-permute-done((f32[512,512]{1,0:T(8,128)}, f32[512,512]{1,0:T(8,128)}, u32[]{:S(2)}, u32[]{:S(2)}) %collective-permute-start.8) | collective-permute-done | bytes 1048608 | tf_op jit(solution)/shard_map/ppermute | solution.py:70
  268.5 3.1 fusion.16
  272.6 2.9 fusion.88
  275.5 3.9 fusion.87
  279.4 3.2 fusion.89
  285.9 3.7 collective-permute-done.10
  295.5 8.5 %collective-permute-done.11 = f32[192,512]{1,0:T(8,128)S(1)} collective-permute-done((f32[192,512]{1,0:T(8,128)S(1)}, f32[192,512]{1,0:T(8,128)S(1)}, u32[]{:S(2)}, u32[]{:S(2)}) %collective-permute-start.11) | collective-permute-done | bytes 393248 | tf_op jit(solution)/shard_map/ppermute | solution.py:70
  304.0 9.1 %collective-permute-done.12 = f32[192,512]{1,0:T(8,128)S(1)} collective-permute-done((f32[192,512]{1,0:T(8,128)S(1)}, f32[192,512]{1,0:T(8,128)S(1)}, u32[]{:S(2)}, u32[]{:S(2)}) %collective-permute-start.12) | collective-permute-done | bytes 393248 | tf_op jit(solution)/shard_map/ppermute | solution.py:70
  313.3 11.9 %collective-permute-start.14 = (f32[48,512]{1,0:T(8,128)S(1)}, f32[48,512]{1,0:T(8,128)S(1)}, u32[]{:S(2)}, u32[]{:S(2)}) collective-permute-start(f32[48,512]{1,0:T(8,128)S(1)} %get-tuple-element.44), channel_id=1, source_target_pairs={{0,2},{1,3},{2,0},{3,1},{4,6},{5,7},{6,4},{7,5},{8,10},{9,11},{10,... | collective-permute-start | bytes 294920 | tf_op jit(solution)/shard_map/ppermute | solution.py:70
  328.4 6.6 %collective-permute-done.15 = f32[48,512]{1,0:T(8,128)S(1)} collective-permute-done((f32[48,512]{1,0:T(8,128)S(1)}, f32[48,512]{1,0:T(8,128)S(1)}, u32[]{:S(2)}, u32[]{:S(2)}) %collective-permute-start.15) | collective-permute-done | bytes 98336 | tf_op jit(solution)/shard_map/ppermute | solution.py:70
  340.9 5.5 %collective-permute-done.18 = f32[48,512]{1,0:T(8,128)S(1)} collective-permute-done((f32[48,512]{1,0:T(8,128)S(1)}, f32[48,512]{1,0:T(8,128)S(1)}, u32[]{:S(2)}, u32[]{:S(2)}) %collective-permute-start.18) | collective-permute-done | bytes 98336 | tf_op jit(solution)/shard_map/ppermute | solution.py:70
  352.0 6.5 %collective-permute-done.20 = f32[192,512]{1,0:T(8,128)S(1)} collective-permute-done((f32[192,512]{1,0:T(8,128)S(1)}, f32[192,512]{1,0:T(8,128)S(1)}, u32[]{:S(2)}, u32[]{:S(2)}) %collective-permute-start.20) | collective-permute-done | bytes 393248 | tf_op jit(solution)/shard_map/ppermute | solution.py:70
  359.2 3.8 collective-permute-done.21
  364.6 3.0 copy.30
  367.6 3.5 fusion.17
  377.8 2.9 convolution_multiply_fusion.2
  386.3 3.0 fusion.20
  389.3 2.5 copy.32
  391.8 3.2 fusion.2
  398.9 2.8 broadcast_multiply_fusion
  409.6 2.8 fusion.26
  (177 shorter events, 102.3 us)
Async XLA Ops:
  7.2 364.0 %copy-start = (f32[512,512]{1,0:T(8,128)S(1)}, f32[512,512]{1,0:T(8,128)}, u32[]{:S(2)}) copy-start(f32[512,512]{1,0:T(8,128)} %param.8) | copy-start | bytes 3145732
  7.2 268.3 %reduce-scatter.2.cloned.1.call-start = ((), (), s32[]{:S(2)}) async-start(), calls=%async_computation.1 | async-start | bytes 9437184 | tf_op jit(solution)/shard_map/reduce_scatter | solution.py:139
  11.5 64.4 %collective-permute-start.3 = (f32[512,512]{1,0:T(8,128)}, f32[512,512]{1,0:T(8,128)}, u32[]{:S(2)}, u32[]{:S(2)}) collective-permute-start(f32[512,512]{1,0:T(8,128)} %get-tuple-element.26), channel_id=1, source_target_pairs={{0,2},{1,3},{2,0},{3,1},{4,6},{5,7},{6,4},{7,5},{8,10},{9,11},{10,... | collective-permute-start | bytes 3145736 | tf_op jit(solution)/shard_map/ppermute | solution.py:70
  14.5 72.2 %collective-permute-start.4 = (f32[512,512]{1,0:T(8,128)}, f32[512,512]{1,0:T(8,128)}, u32[]{:S(2)}, u32[]{:S(2)}) collective-permute-start(f32[512,512]{1,0:T(8,128)} %get-tuple-element.26), channel_id=1, source_target_pairs={{0,4},{1,5},{2,6},{3,7},{4,0},{5,1},{6,2},{7,3},{8,12},{9,13},{10,... | collective-permute-start | bytes 3145736 | tf_op jit(solution)/shard_map/ppermute | solution.py:70
  17.1 72.0 %collective-permute-start.5 = (f32[512,512]{1,0:T(8,128)}, f32[512,512]{1,0:T(8,128)}, u32[]{:S(2)}, u32[]{:S(2)}) collective-permute-start(f32[512,512]{1,0:T(8,128)} %get-tuple-element.26), channel_id=1, source_target_pairs={{0,6},{1,7},{2,4},{3,5},{4,2},{5,3},{6,0},{7,1},{8,14},{9,15},{10,... | collective-permute-start | bytes 3145736 | tf_op jit(solution)/shard_map/ppermute | solution.py:70
  17.1 74.2 %collective-permute-start = (f32[512,512]{1,0:T(8,128)}, f32[512,512]{1,0:T(8,128)}, u32[]{:S(2)}, u32[]{:S(2)}) collective-permute-start(f32[512,512]{1,0:T(8,128)} %get-tuple-element.27), channel_id=1, source_target_pairs={{0,8},{8,0},{16,24},{24,16},{1,9},{9,1},{17,25},{25,17},{2,10},{10... | collective-permute-start | bytes 3145736 | tf_op jit(solution)/shard_map/ppermute | solution.py:70
  18.8 73.8 %collective-permute-start.1 = (f32[512,512]{1,0:T(8,128)}, f32[512,512]{1,0:T(8,128)}, u32[]{:S(2)}, u32[]{:S(2)}) collective-permute-start(f32[512,512]{1,0:T(8,128)} %get-tuple-element.27), channel_id=1, source_target_pairs={{0,16},{8,24},{16,0},{24,8},{1,17},{9,25},{17,1},{25,9},{2,18},{10... | collective-permute-start | bytes 3145736 | tf_op jit(solution)/shard_map/ppermute | solution.py:70
  75.9 24.8 %collective-permute-start.2 = (f32[512,512]{1,0:T(8,128)}, f32[512,512]{1,0:T(8,128)S(1)}, u32[]{:S(2)}, u32[]{:S(2)}) collective-permute-start(f32[512,512]{1,0:T(8,128)} %get-tuple-element.27), channel_id=1, source_target_pairs={{0,24},{8,16},{16,8},{24,0},{1,25},{9,17},{17,9},{25,1},{2,26},{10... | collective-permute-start | bytes 3145736 | tf_op jit(solution)/shard_map/ppermute | solution.py:70
  78.5 12.8 %copy-start.21 = (f32[4,512,512]{2,1,0:T(8,128)S(1)}, f32[4,512,512]{2,1,0:T(8,128)}, u32[]{:S(2)}) copy-start(f32[4,512,512]{2,1,0:T(8,128)} %copy-done.20) | copy-start | bytes 12582916
  132.9 33.2 %collective-permute-start.6 = (f32[4,512,512]{2,1,0:T(8,128)}, f32[4,512,512]{2,1,0:T(8,128)}, u32[]{:S(2)}, u32[]{:S(2)}) collective-permute-start(f32[4,512,512]{2,1,0:T(8,128)} %bitcast_dynamic-update-slice_fusion), channel_id=1, source_target_pairs={{0,1},{1,0},{2,3},{3,2},{4,5},{5,4},{6,7},{7,6},{8,9},{9,8},{10,11... | collective-permute-start | bytes 12582920 | tf_op jit(solution)/shard_map/ppermute | solution.py:70
  220.4 26.3 %collective-permute-start.7 = (f32[512,512]{1,0:T(8,128)}, f32[512,512]{1,0:T(8,128)}, u32[]{:S(2)}, u32[]{:S(2)}) collective-permute-start(f32[512,512]{1,0:T(8,128)} %get-tuple-element.15), channel_id=1, source_target_pairs={{0,8},{8,0},{16,24},{24,16},{1,9},{9,1},{17,25},{25,17},{2,10},{10... | collective-permute-start | bytes 3145736 | tf_op jit(solution)/shard_map/ppermute | solution.py:70
  220.4 48.1 %collective-permute-start.8 = (f32[512,512]{1,0:T(8,128)}, f32[512,512]{1,0:T(8,128)}, u32[]{:S(2)}, u32[]{:S(2)}) collective-permute-start(f32[512,512]{1,0:T(8,128)} %get-tuple-element.17), channel_id=1, source_target_pairs={{0,16},{8,24},{16,0},{24,8},{1,17},{9,25},{17,1},{25,9},{2,18},{10... | collective-permute-start | bytes 3145736 | tf_op jit(solution)/shard_map/ppermute | solution.py:70
  220.6 47.9 %collective-permute-start.9 = (f32[512,512]{1,0:T(8,128)}, f32[512,512]{1,0:T(8,128)}, u32[]{:S(2)}, u32[]{:S(2)}) collective-permute-start(f32[512,512]{1,0:T(8,128)} %get-tuple-element.16), channel_id=1, source_target_pairs={{0,24},{8,16},{16,8},{24,0},{1,25},{9,17},{17,9},{25,1},{2,26},{10... | collective-permute-start | bytes 3145736 | tf_op jit(solution)/shard_map/ppermute | solution.py:70
  223.9 48.7 %copy-start.2 = (f32[2,512,512]{2,1,0:T(8,128)S(1)}, f32[2,512,512]{2,1,0:T(8,128)}, u32[]{:S(2)}) copy-start(f32[2,512,512]{2,1,0:T(8,128)} %param.9) | copy-start | bytes 6291460
  275.5 3.9 copy-start.3
  275.5 3.9 copy-start.13
  285.9 3.8 collective-permute-start.10
  292.0 12.0 %collective-permute-start.11 = (f32[192,512]{1,0:T(8,128)S(1)}, f32[192,512]{1,0:T(8,128)S(1)}, u32[]{:S(2)}, u32[]{:S(2)}) collective-permute-start(f32[192,512]{1,0:T(8,128)S(1)} %get-tuple-element.29), channel_id=1, source_target_pairs={{0,8},{8,0},{16,24},{24,16},{1,9},{9,1},{17,25},{25,17},{2,10},{10... | collective-permute-start | bytes 1179656 | tf_op jit(solution)/shard_map/ppermute | solution.py:70
  293.8 19.3 %collective-permute-start.12 = (f32[192,512]{1,0:T(8,128)S(1)}, f32[192,512]{1,0:T(8,128)S(1)}, u32[]{:S(2)}, u32[]{:S(2)}) collective-permute-start(f32[192,512]{1,0:T(8,128)S(1)} %get-tuple-element.31), channel_id=1, source_target_pairs={{0,16},{8,24},{16,0},{24,8},{1,17},{9,25},{17,1},{25,9},{2,18},{10... | collective-permute-start | bytes 1179656 | tf_op jit(solution)/shard_map/ppermute | solution.py:70
  294.1 19.0 %collective-permute-start.13 = (f32[192,512]{1,0:T(8,128)S(1)}, f32[192,512]{1,0:T(8,128)S(1)}, u32[]{:S(2)}, u32[]{:S(2)}) collective-permute-start(f32[192,512]{1,0:T(8,128)S(1)} %get-tuple-element.30), channel_id=1, source_target_pairs={{0,24},{8,16},{16,8},{24,0},{1,25},{9,17},{17,9},{25,1},{2,26},{10... | collective-permute-start | bytes 1179656 | tf_op jit(solution)/shard_map/ppermute | solution.py:70
  313.3 15.1 %collective-permute-start.14 = (f32[48,512]{1,0:T(8,128)S(1)}, f32[48,512]{1,0:T(8,128)S(1)}, u32[]{:S(2)}, u32[]{:S(2)}) collective-permute-start(f32[48,512]{1,0:T(8,128)S(1)} %get-tuple-element.44), channel_id=1, source_target_pairs={{0,2},{1,3},{2,0},{3,1},{4,6},{5,7},{6,4},{7,5},{8,10},{9,11},{10,... | collective-permute-start | bytes 294920 | tf_op jit(solution)/shard_map/ppermute | solution.py:70
  325.2 9.9 %collective-permute-start.15 = (f32[48,512]{1,0:T(8,128)S(1)}, f32[48,512]{1,0:T(8,128)S(1)}, u32[]{:S(2)}, u32[]{:S(2)}) collective-permute-start(f32[48,512]{1,0:T(8,128)S(1)} %get-tuple-element.46), channel_id=1, source_target_pairs={{0,4},{1,5},{2,6},{3,7},{4,0},{5,1},{6,2},{7,3},{8,12},{9,13},{10,... | collective-permute-start | bytes 294920 | tf_op jit(solution)/shard_map/ppermute | solution.py:70
  326.2 8.9 %collective-permute-start.16 = (f32[48,512]{1,0:T(8,128)S(1)}, f32[48,512]{1,0:T(8,128)S(1)}, u32[]{:S(2)}, u32[]{:S(2)}) collective-permute-start(f32[48,512]{1,0:T(8,128)S(1)} %get-tuple-element.45), channel_id=1, source_target_pairs={{0,6},{1,7},{2,4},{3,5},{4,2},{5,3},{6,0},{7,1},{8,14},{9,15},{10,... | collective-permute-start | bytes 294920 | tf_op jit(solution)/shard_map/ppermute | solution.py:70
  335.1 5.7 %collective-permute-start.17 = (f32[48,512]{1,0:T(8,128)S(1)}, f32[48,512]{1,0:T(8,128)S(1)}, u32[]{:S(2)}, u32[]{:S(2)}) collective-permute-start(f32[48,512]{1,0:T(8,128)S(1)} %get-tuple-element.12), channel_id=1, source_target_pairs={{0,2},{1,3},{2,0},{3,1},{4,6},{5,7},{6,4},{7,5},{8,10},{9,11},{10,... | collective-permute-start | bytes 294920 | tf_op jit(solution)/shard_map/ppermute | solution.py:70
  336.8 9.5 %collective-permute-start.18 = (f32[48,512]{1,0:T(8,128)S(1)}, f32[48,512]{1,0:T(8,128)S(1)}, u32[]{:S(2)}, u32[]{:S(2)}) collective-permute-start(f32[48,512]{1,0:T(8,128)S(1)} %get-tuple-element.12), channel_id=1, source_target_pairs={{0,4},{1,5},{2,6},{3,7},{4,0},{5,1},{6,2},{7,3},{8,12},{9,13},{10,... | collective-permute-start | bytes 294920 | tf_op jit(solution)/shard_map/ppermute | solution.py:70
  337.7 8.6 %collective-permute-start.19 = (f32[48,512]{1,0:T(8,128)S(1)}, f32[48,512]{1,0:T(8,128)S(1)}, u32[]{:S(2)}, u32[]{:S(2)}) collective-permute-start(f32[48,512]{1,0:T(8,128)S(1)} %get-tuple-element.12), channel_id=1, source_target_pairs={{0,6},{1,7},{2,4},{3,5},{4,2},{5,3},{6,0},{7,1},{8,14},{9,15},{10,... | collective-permute-start | bytes 294920 | tf_op jit(solution)/shard_map/ppermute | solution.py:70
  346.4 12.1 %collective-permute-start.20 = (f32[192,512]{1,0:T(8,128)S(1)}, f32[192,512]{1,0:T(8,128)S(1)}, u32[]{:S(2)}, u32[]{:S(2)}) collective-permute-start(f32[192,512]{1,0:T(8,128)S(1)} %bitcast.265), channel_id=1, source_target_pairs={{0,8},{8,0},{16,24},{24,16},{1,9},{9,1},{17,25},{25,17},{2,10},{10... | collective-permute-start | bytes 1179656 | tf_op jit(solution)/shard_map/ppermute | solution.py:70
  347.0 16.1 %collective-permute-start.21 = (f32[192,512]{1,0:T(8,128)S(1)}, f32[192,512]{1,0:T(8,128)S(1)}, u32[]{:S(2)}, u32[]{:S(2)}) collective-permute-start(f32[192,512]{1,0:T(8,128)S(1)} %bitcast.266), channel_id=1, source_target_pairs={{0,16},{8,24},{16,0},{24,8},{1,17},{9,25},{17,1},{25,9},{2,18},{10... | collective-permute-start | bytes 1179656 | tf_op jit(solution)/shard_map/ppermute | solution.py:70
  348.1 15.7 %collective-permute-start.22 = (f32[192,512]{1,0:T(8,128)S(1)}, f32[192,512]{1,0:T(8,128)S(1)}, u32[]{:S(2)}, u32[]{:S(2)}) collective-permute-start(f32[192,512]{1,0:T(8,128)S(1)} %bitcast.267), channel_id=1, source_target_pairs={{0,24},{8,16},{16,8},{24,0},{1,25},{9,17},{17,9},{25,1},{2,26},{10... | collective-permute-start | bytes 1179656 | tf_op jit(solution)/shard_map/ppermute | solution.py:70
  367.6 3.5 copy-start.10
  367.6 9.3 %collective-permute-start.23 = (f32[768,512]{0,1:T(8,128)}, f32[768,512]{0,1:T(8,128)S(1)}, u32[]{:S(2)}, u32[]{:S(2)}) collective-permute-start(f32[768,512]{0,1:T(8,128)} %copy.30), channel_id=1, source_target_pairs={{0,1},{1,0},{2,3},{3,2},{4,5},{5,4},{6,7},{7,6},{8,9},{9,8},{10,11... | collective-permute-start | bytes 4718600 | tf_op jit(solution)/shard_map/ppermute | solution.py:70
  391.8 3.2 copy-start.12
  (20 other events, 41.2 us)
Sparse Core Ops, SparseCore 0:
  133.0 100.9 reduce-scatter.1
